TPU v7x, 256 devices: a whole 4x4x8 slice. The times are simulated.
256 devices in a mesh: src: 64 (over x, y, z_hi), blk: 4 (over z_lo, core).
Axes of the slice: x: 4, y: 4, z: 8 (z_hi: 4, z_lo: 2; z = z_hi * 2 + z_lo), core: 2. Of those that a mesh axis runs over, the one named last changes fastest.
Arguments:
- sources: bfloat16 [524288, 1024], P(('src', 'blk')), may hold values from -18 to 18
- targets: bfloat16 [1024, 1024], P('blk'), may hold values from -6 to 6
- log_src: float32 [524288], P(('src', 'blk')), may hold values from -1 to 2.1
- log_tgt: float32 [1024], P('blk'), may hold values from -1 to 1
- potential: float32 [1024], P('blk'), may hold values from -60 to 60
Outputs:
- source_potential: float32 [524288], P(('src', 'blk'))
- target_potential: float32 [1024], P('blk')
All inputs are finite; a program needn't handle non-finite values.
Results may differ from a plain program's by a relative error of at most 0.0003.
Values may be sent and summed in bfloat16 or wider, within the bound.
A program may use at most 64 MiB of HBM per device.

v0:
```python
import math

import jax
import jax.numpy as jnp
from jax import lax
from jax.sharding import PartitionSpec as P

EPSILON = 0.5


def shifted(block, axis, distance):
    devices = range(lax.axis_size(axis))
    route = [((i - distance) % len(devices), i) for i in devices]
    return lax.ppermute(block, axis, route)


def tile_cost(sources, src_norms, moving):
    tgt_norms = jnp.sum(jnp.square(moving.astype(jnp.float32)), axis=1)
    inner = jnp.dot(sources, moving.T, preferred_element_type=jnp.float32)
    width = sources.shape[1]
    return (src_norms[:, None] + tgt_norms[None, :] - 2.0 * inner) / math.sqrt(
        width
    ) - 2.0 * math.sqrt(width)


def combine_pairs(left_pair, right_pair):
    merged = jnp.maximum(left_pair[0], right_pair[0])
    total = left_pair[1] * jnp.exp(left_pair[0] - merged) + right_pair[1] * jnp.exp(
        right_pair[0] - merged
    )
    return (merged, total)


def local(sources, targets, log_src, log_tgt, potential):
    cycle_size = lax.axis_size("blk")
    my_index = lax.axis_index("blk")
    tgt_rows = targets.shape[0]
    all_rows = tgt_rows * cycle_size
    src_norms = jnp.sum(jnp.square(sources.astype(jnp.float32)), axis=1)
    table = lax.all_gather(jnp.stack([potential, log_tgt]), "blk", axis=1, tiled=True)
    bias_all = table[1] + table[0] / EPSILON
    owners = []
    row_pair = None
    moving = targets
    for turn_number in range(cycle_size):
        owner = (my_index - turn_number) % cycle_size
        cost = tile_cost(sources, src_norms, moving)
        bias = lax.dynamic_slice_in_dim(bias_all, owner * tgt_rows, tgt_rows)
        scores = bias[None, :] - cost / EPSILON
        top = jnp.max(scores, axis=1)
        total = jnp.sum(jnp.exp(scores - top[:, None]), axis=1)
        row_pair = (top, total) if row_pair is None else combine_pairs(row_pair, (top, total))
        owners.append(owner)
        if turn_number + 1 < cycle_size:
            moving = shifted(moving, "blk", 1)
    source_potential = -EPSILON * (row_pair[0] + jnp.log(row_pair[1]))
    col_max = jnp.zeros((all_rows,), jnp.float32)
    col_sum = jnp.zeros((all_rows,), jnp.float32)
    moving = targets
    for turn_number in range(cycle_size):
        cost = tile_cost(sources, src_norms, moving)
        col_scores = log_src[:, None] + (source_potential[:, None] - cost) / EPSILON
        col_top = jnp.max(col_scores, axis=0)
        col_total = jnp.sum(jnp.exp(col_scores - col_top[None, :]), axis=0)
        col_top, col_total = (col_top, col_total)
        col_max = lax.dynamic_update_slice_in_dim(
            col_max, col_top, owners[turn_number] * tgt_rows, 0
        )
        col_sum = lax.dynamic_update_slice_in_dim(
            col_sum, col_total, owners[turn_number] * tgt_rows, 0
        )
        if turn_number + 1 < cycle_size:
            moving = shifted(moving, "blk", 1)
    global_max = lax.pmax(col_max, ("src", "blk"))
    global_sum = lax.psum(col_sum * jnp.exp(col_max - global_max), ("src", "blk"))
    target_all = -EPSILON * (global_max + jnp.log(global_sum))
    target_potential = lax.dynamic_slice_in_dim(target_all, my_index * tgt_rows, tgt_rows)
    return (source_potential, target_potential)


def solution(mesh):
    placed = (P(("src", "blk"), None), P("blk", None), P(("src", "blk")), P("blk"), P("blk"))
    return jax.shard_map(
        local, mesh=mesh, in_specs=placed, out_specs=(P(("src", "blk")), P("blk")), check_vma=False
    )
```

profile of v0, /device:TPU:1, one launch (start us, length us, event | category | flops | bytes accessed | tf_op | source)
XLA Modules:
  0.0 200.9 jit_solution(14015525570847224733)
XLA Ops:
  0.6 3.1 %collective-permute-start = (bf16[256,1024]{1,0:T(8,128)(2,1)}, bf16[256,1024]{1,0:T(8,128)(2,1)S(1)}, u32[]{:S(2)}, u32[]{:S(2)}) collective-permute-start(bf16[256,1024]{1,0:T(8,128)(2,1)} %param.6), channel_id=1, source_target_pairs={{3,0},{0,1},{1,2},{2,3},{7,4},{4,5},{5,6},{6,7},{11,8},{8,9},{9,10... | collective-permute-start | bytes 1572872 | tf_op jit(solution)/shard_map/ppermute | solution.py:14
  3.7 1.3 multiply_reduce_fusion.4
  5.0 0.7 pad_maximum_fusion
  5.7 7.5 %all_gather.3 = f32[2,1024]{1,0:T(2,128)S(1)} all-gather(f32[2,256]{1,0:T(2,128)S(1)} %pad_maximum_fusion), channel_id=1, replica_groups=mesh['src'=64,'blk'=4] {'blk'}, dimensions={1}, use_global_device_ids=true | all-gather | bytes 10240 | tf_op jit(solution)/shard_map/all_gather | solution.py:40
  13.2 3.1 %multiply_reduce_fusion = f32[2048]{0:T(1024)S(1)} fusion(bf16[2048,1024]{1,0:T(8,128)(2,1)} %param.5), kind=kLoop, calls=%fused_computation | loop fusion | flops 6289408 | bytes 4202496 | tf_op jit(solution)/shard_map/reduce_sum | solution.py:39
  16.4 4.0 %fusion.3 = (f32[2048]{0:T(1024)S(1)}, f32[2048,256]{1,0:T(8,128)S(1)}) fusion(f32[256]{0:T(256)S(1)} %bitcast.20, bf16[2048,1024]{1,0:T(8,128)(2,1)} %param.5, bf16[256,1024]{1,0:T(8,128)(2,1)S(1)} %copy-done.4, f32[256]{0:T(256)S(1)} %multiply_reduce_fusion.4, f32[2048]{0:T(1024)S(1)} %multiply_reduce_fusion), kind=kOutput, calls=%fused_computation.27 | convolution fusion | flops 1077934080 | bytes 6834176 | tf_op jit(solution)/shard_map/dot_general | solution.py:19
  20.4 0.8 exponential_reduce_fusion.7
  21.4 0.2 multiply_reduce_fusion.3
  21.6 1.8 fusion.4
  23.4 0.8 exponential_reduce_fusion.6
  24.2 3.3 %collective-permute-done.1 = bf16[256,1024]{1,0:T(8,128)(2,1)S(1)} collective-permute-done((bf16[256,1024]{1,0:T(8,128)(2,1)S(1)}, bf16[256,1024]{1,0:T(8,128)(2,1)S(1)}, u32[]{:S(2)}, u32[]{:S(2)}) %collective-permute-start.1) | collective-permute-done | bytes 524320 | tf_op jit(solution)/shard_map/ppermute | solution.py:14
  27.5 2.5 %collective-permute-start.2 = (bf16[256,1024]{1,0:T(8,128)(2,1)S(1)}, bf16[256,1024]{1,0:T(8,128)(2,1)S(1)}, u32[]{:S(2)}, u32[]{:S(2)}) collective-permute-start(bf16[256,1024]{1,0:T(8,128)(2,1)S(1)} %collective-permute-done.1), channel_id=1, source_target_pairs={{3,0},{0,1},{1,2},{2,3},{7,4},{4,5},{5,6},{6,7},{11,8},{8,9},{9,10... | collective-permute-start | bytes 1572872 | tf_op jit(solution)/shard_map/ppermute | solution.py:14
  30.0 0.2 multiply_reduce_fusion.2
  30.2 1.8 fusion.5
  32.0 0.8 exponential_reduce_fusion.5
  32.8 3.3 %collective-permute-done.2 = bf16[256,1024]{1,0:T(8,128)(2,1)S(1)} collective-permute-done((bf16[256,1024]{1,0:T(8,128)(2,1)S(1)}, bf16[256,1024]{1,0:T(8,128)(2,1)S(1)}, u32[]{:S(2)}, u32[]{:S(2)}) %collective-permute-start.2) | collective-permute-done | bytes 524320 | tf_op jit(solution)/shard_map/ppermute | solution.py:14
  36.1 0.2 multiply_reduce_fusion.1
  36.3 1.8 fusion.6
  38.1 0.8 exponential_reduce_fusion.4
  39.0 0.7 fusion.10
  39.7 0.2 dynamic_update_slice.24
  40.0 3.6 %exponential_reduce_fusion = (f32[256]{0:T(256)S(1)}, f32[256]{0:T(256)S(1)}, f32[256]{0:T(256)S(1)}, f32[256]{0:T(256)S(1)}) fusion(f32[2048,256]{1,0:T(8,128)} %copy-done.2, f32[256]{0:T(256)S(1)} %get-tuple-element.8, f32[2048]{0:T(1024)S(1)} %add_multiply_fusion, f32[2048]{0:T(1024)S(1)} %copy-done.6, f32[2048,256]{1,0:T(8,128)} %copy-done, ...), kind=kLoop, calls=%fused_computation.8 | loop fusion | flops 9436160 | bytes 8411136 | tf_op jit(solution)/shard_map/reduce_sum | solution.py:64
  43.6 0.2 dynamic_update_slice.25
  43.9 2.7 %exponential_reduce_fusion.1 = (f32[256]{0:T(256)S(1)}, f32[256]{0:T(256)S(1)}) fusion(f32[2048,256]{1,0:T(8,128)} %copy-done.1, f32[256]{0:T(256)S(1)} %get-tuple-element.4, f32[2048]{0:T(1024)S(1)} %add_multiply_fusion, f32[2048]{0:T(1024)S(1)} %copy-done.6, f32[256]{0:T(256)S(1)} %get-tuple-element.3, f32[2048,256]{1,0:T(8,128)} %copy-done), kind=kLoop, calls=%fused_computation.9 | loop fusion | flops 5242368 | bytes 4214784 | tf_op jit(solution)/shard_map/reduce_sum | solution.py:64
  46.6 0.2 dynamic_update_slice.26
  46.9 0.2 dynamic_update_slice.27
  47.1 79.7 %pmax.7 = f32[1024]{0:T(1024)S(1)} all-reduce(f32[1024]{0:T(1024)S(1)} %dynamic_update_slice.27), channel_id=1, replica_groups=mesh['src'=64,'blk'=4] {'src','blk'}, use_global_device_ids=true, to_apply=%region_17.18 | all-reduce | flops 1024 | bytes 8192 | tf_op jit(solution)/shard_map/pmax | solution.py:74
  126.9 0.2 dynamic_update_slice.29
  127.1 0.2 dynamic_update_slice.30
  127.3 0.2 dynamic_update_slice.31
  127.6 72.7 %psum.7 = f32[1024]{0:T(1024)S(1)} all-reduce(f32[1024]{0:T(1024)S(1)} %exponential_multiply_fusion), channel_id=1, replica_groups=mesh['src'=64,'blk'=4] {'src','blk'}, use_global_device_ids=true, to_apply=%region_22.23 | all-reduce | flops 1024 | bytes 8192 | tf_op jit(solution)/shard_map/psum | solution.py:75
  200.2 0.6 dynamic_slice.31
  (24 shorter events, 0.5 us)
Async XLA Ops:
  0.6 20.6 %collective-permute-start = (bf16[256,1024]{1,0:T(8,128)(2,1)}, bf16[256,1024]{1,0:T(8,128)(2,1)S(1)}, u32[]{:S(2)}, u32[]{:S(2)}) collective-permute-start(bf16[256,1024]{1,0:T(8,128)(2,1)} %param.6), channel_id=1, source_target_pairs={{3,0},{0,1},{1,2},{2,3},{7,4},{4,5},{5,6},{6,7},{11,8},{8,9},{9,10... | collective-permute-start | bytes 1572872 | tf_op jit(solution)/shard_map/ppermute | solution.py:14
  13.2 3.2 %copy-start.4 = (bf16[256,1024]{1,0:T(8,128)(2,1)S(1)}, bf16[256,1024]{1,0:T(8,128)(2,1)}, u32[]{:S(2)}) copy-start(bf16[256,1024]{1,0:T(8,128)(2,1)} %param.6) | copy-start | bytes 1572868
  16.4 5.1 %copy-start.3 = (bf16[2048,1024]{1,0:T(8,128)(2,1)S(1)}, bf16[2048,1024]{1,0:T(8,128)(2,1)}, u32[]{:S(2)}) copy-start(bf16[2048,1024]{1,0:T(8,128)(2,1)} %param.5) | copy-start | bytes 12582916
  21.2 6.3 %collective-permute-start.1 = (bf16[256,1024]{1,0:T(8,128)(2,1)S(1)}, bf16[256,1024]{1,0:T(8,128)(2,1)S(1)}, u32[]{:S(2)}, u32[]{:S(2)}) collective-permute-start(bf16[256,1024]{1,0:T(8,128)(2,1)S(1)} %collective-permute-done), channel_id=1, source_target_pairs={{3,0},{0,1},{1,2},{2,3},{7,4},{4,5},{5,6},{6,7},{11,8},{8,9},{9,10... | collective-permute-start | bytes 1572872 | tf_op jit(solution)/shard_map/ppermute | solution.py:14
  23.3 8.6 %copy-start = (f32[2048,256]{1,0:T(8,128)}, f32[2048,256]{1,0:T(8,128)S(1)}, u32[]{:S(2)}) copy-start(f32[2048,256]{1,0:T(8,128)S(1)} %get-tuple-element.19) | copy-start | bytes 6291460
  27.5 8.6 %collective-permute-start.2 = (bf16[256,1024]{1,0:T(8,128)(2,1)S(1)}, bf16[256,1024]{1,0:T(8,128)(2,1)S(1)}, u32[]{:S(2)}, u32[]{:S(2)}) collective-permute-start(bf16[256,1024]{1,0:T(8,128)(2,1)S(1)} %collective-permute-done.1), channel_id=1, source_target_pairs={{3,0},{0,1},{1,2},{2,3},{7,4},{4,5},{5,6},{6,7},{11,8},{8,9},{9,10... | collective-permute-start | bytes 1572872 | tf_op jit(solution)/shard_map/ppermute | solution.py:14
  32.0 6.1 %copy-start.1 = (f32[2048,256]{1,0:T(8,128)}, f32[2048,256]{1,0:T(8,128)S(1)}, u32[]{:S(2)}) copy-start(f32[2048,256]{1,0:T(8,128)S(1)} %get-tuple-element.17) | copy-start | bytes 6291460
  38.1 1.6 copy-start.2
  38.1 0.9 copy-start.6
  39.0 4.9 %copy-start.5 = (f32[2048]{0:T(1024)}, f32[2048]{0:T(1024)S(1)}, u32[]{:S(2)}) copy-start(f32[2048]{0:T(1024)S(1)} %add_multiply_fusion) | copy-start | bytes 24580
where the time goes:
time: 201 us
  blocking collectives  160 us (80%)
  other arithmetic  16 us (8%)
  matrix products  9.28 us (5%)
  waiting for transfers between devices  6.67 us (3%)
  starting transfers between devices  5.76 us (3%)
  local copies, waits for them, and re-layouts  2.44 us (1%)
    pmax x1, blocking collectives, local(): global_max = lax.pmax(col_max, ('src', 'blk'))  79.7 us
    psum x1, blocking collectives, local(): lax.psum(col_sum * jnp.exp(col_max - global_max), ('src', 'blk'))  72.7 us
    dot_general x4, matrix products, tile_cost(): inner = jnp.dot(sources, moving.T, preferred_element_type=jnp.float32)  9.28 us
    all_gather x1, blocking collectives, local(): lax.all_gather(jnp.stack([potential, log_tgt]), 'blk', axis=1, tiled=True)  7.53 us
    ppermute x3, waiting for transfers between devices, shifted(): return lax.ppermute(block, axis, route)  6.67 us
    reduce_sum x2, other arithmetic, local(): col_total = jnp.sum(jnp.exp(col_scores - col_top[None, :]), axis=0)  6.38 us
    ppermute x3, starting transfers between devices, shifted(): return lax.ppermute(block, axis, route)  5.76 us
  transfers between devices with their start and end apart: 3, of which 2 were waited for; matrix products, arithmetic and copies ran while one was open for 8% of the time, Pallas kernels for 0%

commit v1 on v0

v1 whole, which is shorter than its diff:
```python
import functools
import math

import jax
import jax.numpy as jnp
from jax import lax
from jax.experimental import pallas as pl
from jax.experimental.pallas import tpu as pltpu
from jax.sharding import PartitionSpec as P

MESH = pl.DeviceIdType.MESH
LOG2E = math.log2(math.e)
LN2 = math.log(2.0)
F32 = jnp.float32

ROWS = 2048
COLS = 1024
BLOCK = 256
WIDTH = 1024
TILE = 128
SIDE = 4
PIECES = 2
PART = BLOCK // 2 // PIECES


def dot_t(left, right):
    return lax.dot_general(left, right, (((1,), (1,)), ((), ())), preferred_element_type=F32)


def fold_lanes(op, value):
    while value.shape[1] > TILE:
        half = value.shape[1] // 2
        value = op(value[:, :half], value[:, half:])
    return value


def kernel(
    sources,
    targets,
    log_src,
    log_tgt,
    potential,
    src_out,
    tgt_out,
    src_v,
    near_t,
    far_t,
    bias_v,
    weight_v,
    row_bias,
    wide_bias,
    norms,
    scores,
    row_max,
    row_sum,
    shift,
    col_max,
    col_sum,
    col_log,
    line_in,
    line_out,
    plane_in,
    load_sem,
    send_sem,
    recv_sem,
    reduce_sem,
):
    src = lax.axis_index("src")
    blk = lax.axis_index("blk")
    x, y, z_hi = src // (SIDE * SIDE), (src // SIDE) % SIDE, src % SIDE
    z_lo, core = blk // 2, blk % 2
    z = z_hi * 2 + z_lo

    def device(to_x, to_y, to_z, to_core):
        return ((to_x * SIDE + to_y) * SIDE + to_z // 2, (to_z % 2) * 2 + to_core)

    def line(step, to_core):
        return device(x, y, (z + step) % (2 * SIDE), to_core)

    def plane(step, to_core):
        return device((x + step // SIDE) % SIDE, (y + step % SIDE) % SIDE, z, to_core)

    sibling = line(0, 1 - core)
    above, below = line(1, core), line(2 * SIDE - 1, core)

    loads = []

    def load(from_ref, to_ref):
        copy = pltpu.make_async_copy(from_ref, to_ref, load_sem.at[len(loads)])
        copy.start()
        loads.append(copy)
        return copy

    own_rows = pl.ds(pl.multiple_of(core * BLOCK, BLOCK), BLOCK)
    sib_rows = pl.ds(pl.multiple_of((1 - core) * BLOCK, BLOCK), BLOCK)
    load_t = load(targets, near_t.at[own_rows])
    load_p = load(potential, bias_v.at[0:2])
    load_l = load(log_tgt, bias_v.at[8:10])
    load_w = load(log_src, weight_v)
    quarter = ROWS // 4
    load_s = [
        load(sources.at[n * quarter : (n + 1) * quarter], src_v.at[n * quarter : (n + 1) * quarter])
        for n in range(4)
    ]

    barrier = pltpu.get_barrier_semaphore()

    def greet(peers):
        for peer in peers:
            pl.semaphore_signal(barrier, inc=1, device_id=peer, device_id_type=MESH)
        pl.semaphore_wait(barrier, len(peers))

    @pl.when(core == 0)
    def _():
        greet(
            [sibling, above, below]
            + [line(step, 1) for step in range(1, 2 * SIDE)]
            + [plane(step, 1) for step in range(1, SIDE * SIDE)]
        )

    @pl.when(core == 1)
    def _():
        greet(
            [sibling]
            + [line(step, to) for step in range(1, 2 * SIDE) for to in range(2)]
            + [plane(step, to) for step in range(1, SIDE * SIDE) for to in range(2)]
        )

    sends = []

    def send(from_ref, to_ref, number, peer):
        copy = pltpu.make_async_remote_copy(
            src_ref=from_ref,
            dst_ref=to_ref,
            send_sem=send_sem.at[number],
            recv_sem=recv_sem.at[number],
            device_id=peer,
            device_id_type=MESH,
        )
        copy.start()
        sends.append(copy)
        return copy

    load_t.wait()
    core_rows = core * BLOCK
    up, down, pass_up, pass_down = [], [], [], []
    for piece in range(PIECES):
        low = pl.ds(pl.multiple_of(core_rows + piece * PART, PART), PART)
        high = pl.ds(pl.multiple_of(core_rows + BLOCK // 2 + piece * PART, PART), PART)
        land_low = pl.ds(pl.multiple_of(core * 2 * PART, PART), PART)
        land_high = pl.ds(pl.multiple_of(core * 2 * PART + PART, PART), PART)
        up.append(send(near_t.at[low], far_t.at[piece, land_low], 4 * piece, above))
        down.append(send(near_t.at[high], far_t.at[piece, land_high], 4 * piece + 1, below))
    near = send(near_t.at[own_rows], near_t.at[own_rows], 4 * PIECES, sibling)

    load_p.wait()
    load_l.wait()
    for half in range(2):
        rows = pl.ds(pl.multiple_of(core_rows + half * TILE, TILE), TILE)
        block = near_t[rows, :].astype(F32)
        tgt_norms = jnp.sum(fold_lanes(jnp.add, block * block).T, axis=0, keepdims=True)
        bias = bias_v[8 + half : 9 + half, :] + 2.0 * bias_v[half : half + 1, :]
        row_bias[pl.ds(core * 2 + half, 1), :] = (bias - tgt_norms / 16.0) * LOG2E
    own_bias = row_bias.at[pl.ds(core * 2, 2)]
    far_bias = row_bias.at[pl.ds(4 + core * 2, 2)]
    bias_near = send(own_bias, own_bias, 4 * PIECES + 1, sibling)
    bias_far = send(own_bias, far_bias, 4 * PIECES + 2, above)

    def widen(slot):
        for half in range(2):
            row = jnp.broadcast_to(row_bias[pl.ds(slot * 2 + half, 1), :], (TILE, TILE))
            wide_bias[pl.ds(pl.multiple_of(slot * BLOCK + half * TILE, TILE), TILE), :] = row.T

    def row_pass(moving, segments, number, waits=()):
        bias = [wide_bias[rows, :] for rows in segments]
        bias = bias[0] if len(bias) == 1 else jnp.concatenate(bias, axis=0)
        length = bias.shape[0] // len(segments)
        for part in range(4):
            if waits:
                waits[part].wait()
            inner = dot_t(moving, src_v[part * quarter : (part + 1) * quarter, :])
            for tile in range(quarter // TILE):
                lanes = pl.ds(part * quarter + tile * TILE, TILE)
                value = inner[:, tile * TILE : (tile + 1) * TILE] * (LOG2E / 8.0) + bias
                for at, rows in enumerate(segments):
                    scores[rows, lanes] = value[at * length : (at + 1) * length, :]
                deep = value.reshape(-1, 8, TILE)
                top = jnp.max(deep, axis=0)
                row_max[number * 8 : number * 8 + 8, lanes] = top
                row_sum[number * 8 : number * 8 + 8, lanes] = jnp.sum(jnp.exp2(deep - top[None]), axis=0)

    widen(core)
    row_pass(near_t[own_rows, :], [own_rows], 0, load_s)
    near.wait_recv()
    bias_near.wait_recv()
    widen(1 - core)
    row_pass(near_t[sib_rows, :], [sib_rows], 1)

    bias_far.wait_recv()
    bias_pass = send(far_bias, far_bias, 4 * PIECES + 3, sibling)
    for piece in range(PIECES):
        up[piece].wait_recv()
        down[piece].wait_recv()
        land = far_t.at[piece, pl.ds(pl.multiple_of(core * 2 * PART, 2 * PART), 2 * PART)]
        passed = send(land, land, 4 * piece + 2, sibling)
        if piece == 0:
            for tile in range(ROWS // TILE):
                block = src_v[tile * TILE : (tile + 1) * TILE, :].astype(F32)
                norms[tile : tile + 1, :] = jnp.sum(fold_lanes(jnp.add, block * block).T, axis=0, keepdims=True)
            bias_pass.wait_recv()
            widen(2)
            widen(3)
        passed.wait_recv()
        segments = [
            pl.ds(2 * BLOCK + of_core * BLOCK + half * (BLOCK // 2) + piece * PART, PART)
            for of_core in range(2)
            for half in range(2)
        ]
        row_pass(far_t[piece], segments, 2 + piece)

    load_w.wait()
    peaks = row_max[...].reshape(2 + PIECES, 8, ROWS)
    peak = jnp.max(peaks, axis=0)
    total = jnp.sum(row_sum[...].reshape(2 + PIECES, 8, ROWS) * jnp.exp2(peaks - peak[None]), axis=0)
    top = jnp.max(peak, axis=0, keepdims=True)
    row_log = top + jnp.log2(jnp.sum(total * jnp.exp2(peak - top), axis=0, keepdims=True))
    weights = jnp.concatenate([weight_v[n : n + 1, :] for n in range(ROWS // TILE)], axis=1)
    shift[...] = jnp.broadcast_to(weights * LOG2E - row_log, (8, ROWS))
    for tile in range(ROWS // TILE):
        src_out[tile : tile + 1, :] = (
            norms[tile : tile + 1, :] / 32.0 - 64.0 - (0.5 * LN2) * row_log[:, tile * TILE : (tile + 1) * TILE]
        )

    for block in range(COLS // TILE):
        for group in range(TILE // 8):
            rows = pl.ds(block * TILE + group * 8, 8)
            value = scores[rows, :] + shift[...]
            peak = fold_lanes(jnp.maximum, value)
            deep = jnp.concatenate([peak] * (ROWS // TILE), axis=1)
            col_max[rows, :] = peak
            col_sum[rows, :] = fold_lanes(jnp.add, jnp.exp2(value - deep))
        rows = pl.ds(block * TILE, TILE)
        peaks = col_max[rows, :].T
        peak = jnp.max(peaks, axis=0, keepdims=True)
        total = jnp.sum(col_sum[rows, :].T * jnp.exp2(peaks - peak), axis=0, keepdims=True)
        col_log[block : block + 1, :] = peak + jnp.log2(total)

    def reduce_send(from_ref, to_ref, stage, peer):
        copy = pltpu.make_async_remote_copy(
            src_ref=from_ref,
            dst_ref=to_ref,
            send_sem=reduce_sem.at[2 * stage],
            recv_sem=reduce_sem.at[2 * stage + 1],
            device_id=peer,
            device_id_type=MESH,
        )
        copy.start()
        return copy

    def arrived(ref, stage):
        pltpu.make_async_copy(ref, ref, reduce_sem.at[2 * stage + 1]).wait()

    def left(ref, stage):
        pltpu.make_async_copy(ref, ref, reduce_sem.at[2 * stage]).wait()

    def merge(value, rows):
        deep = value.reshape(-1, 8, TILE)
        peak = jnp.max(deep, axis=0)
        total = jnp.sum(jnp.exp2(deep - peak[None]), axis=0)
        parts = [slice(n, n + rows) for n in range(0, 8, rows)]
        top = functools.reduce(jnp.maximum, [peak[p] for p in parts])
        return top + jnp.log2(sum(total[p] * jnp.exp2(peak[p] - top) for p in parts))

    for step in range(1, 2 * SIDE):
        part = col_log.at[4 * (step % 2) : 4 * (step % 2) + 4]
        slot = pl.ds(pl.multiple_of(8 * step + 4 * core, 4), 4)
        reduce_send(part, line_in.at[slot], 0, line(step, 1))

    @pl.when(core == 0)
    def _():
        reduce_send(col_log.at[0:4], line_in.at[0:4], 0, sibling)
        arrived(plane_in, 1)
        left(line_in.at[0:32], 0)

    @pl.when(core == 1)
    def _():
        line_in[4:8, :] = col_log[0:4, :]
        arrived(line_in.at[0:60], 0)
        line_out[0:4, :] = merge(line_in[...], 4)
        for step in range(1, SIDE * SIDE):
            for to in range(2):
                reduce_send(
                    line_out.at[2 * to : 2 * to + 2], plane_in.at[2 * step : 2 * step + 2], 1, plane(step, to)
                )
        reduce_send(line_out.at[0:2], plane_in.at[0:2], 1, sibling)
        plane_in[0:2, :] = line_out[2:4, :]
        arrived(plane_in.at[2:32], 1)
        left(line_in.at[0:28], 0)
        left(line_in.at[0:62], 1)

    tgt_out[...] = bias_v[0:2, :] + 0.5 * bias_v[8:10, :] - (0.5 * LN2) * merge(plane_in[...], 2)

    for copy in sends:
        copy.wait_send()


def local(sources, targets, log_src, log_tgt, potential):
    anywhere = pl.BlockSpec(memory_space=pl.ANY)
    vmem = pl.BlockSpec(memory_space=pltpu.VMEM)
    src_out, tgt_out = pl.pallas_call(
        kernel,
        out_shape=[
            jax.ShapeDtypeStruct((ROWS // TILE, TILE), F32),
            jax.ShapeDtypeStruct((BLOCK // TILE, TILE), F32),
        ],
        in_specs=[anywhere] * 5,
        out_specs=[vmem] * 2,
        scratch_shapes=[
            pltpu.VMEM((ROWS, WIDTH), jnp.bfloat16),
            pltpu.VMEM((2 * BLOCK, WIDTH), jnp.bfloat16),
            pltpu.VMEM((PIECES, 4 * PART, WIDTH), jnp.bfloat16),
            pltpu.VMEM((16, TILE), F32),
            pltpu.VMEM((ROWS // TILE, TILE), F32),
            pltpu.VMEM((8, TILE), F32),
            pltpu.VMEM((COLS, TILE), F32),
            pltpu.VMEM((ROWS // TILE, TILE), F32),
            pltpu.VMEM((COLS, ROWS), F32),
            pltpu.VMEM((8 * (2 + PIECES), ROWS), F32),
            pltpu.VMEM((8 * (2 + PIECES), ROWS), F32),
            pltpu.VMEM((8, ROWS), F32),
            pltpu.VMEM((COLS, TILE), F32),
            pltpu.VMEM((COLS, TILE), F32),
            pltpu.VMEM((8, TILE), F32),
            pltpu.VMEM((64, TILE), F32),
            pltpu.VMEM((8, TILE), F32),
            pltpu.VMEM((32, TILE), F32),
            pltpu.SemaphoreType.DMA((8,)),
            pltpu.SemaphoreType.DMA((4 * PIECES + 4,)),
            pltpu.SemaphoreType.DMA((4 * PIECES + 4,)),
            pltpu.SemaphoreType.DMA((4,)),
        ],
        compiler_params=pltpu.CompilerParams(
            collective_id=0, has_side_effects=True, vmem_limit_bytes=56 * 2**20
        ),
        cost_estimate=pl.CostEstimate(
            flops=2 * ROWS * COLS * WIDTH,
            bytes_accessed=2 * WIDTH * (ROWS + COLS),
            transcendentals=2 * ROWS * COLS,
        ),
    )(
        sources,
        targets,
        log_src.reshape(ROWS // TILE, TILE),
        log_tgt.reshape(BLOCK // TILE, TILE),
        potential.reshape(BLOCK // TILE, TILE),
    )
    return src_out.reshape(ROWS), tgt_out.reshape(BLOCK)


def solution(mesh):
    placed = (P(("src", "blk"), None), P("blk", None), P(("src", "blk")), P("blk"), P("blk"))
    return jax.shard_map(
        local, mesh=mesh, in_specs=placed, out_specs=(P(("src", "blk")), P("blk")), check_vma=False
    )
```

time: 201 us -> 39.7 us (0.20)
  blocking collectives: 160 us -> 0 us
  Pallas kernels: 0 us -> 36.3 us
  other arithmetic: 16 us -> 0 us
  matrix products: 9.28 us -> 0 us
  waiting for transfers between devices: 6.67 us -> 0 us
  starting transfers between devices: 5.76 us -> 0 us
    pmax x1 -> x0, blocking collectives: 79.7 us -> none  [local(): global_max = lax.pmax(col_max, ('src', 'blk'))]
    psum x1 -> x0, blocking collectives: 72.7 us -> none  [local(): lax.psum(col_sum * jnp.exp(col_max - global_max), ('src', 'blk'))]
    pallas_call x0 -> x1, Pallas kernels: none -> 36.3 us  [local(): pl.pallas_call(kernel, out_shape=[jax.ShapeDtypeStruct((ROWS // TILE, TIL...]
    reduce_sum x11 -> x0, other arithmetic: 14.5 us -> none  [the longest x2 6.38 us: local(): col_total = jnp.sum(jnp.exp(col_scores - col_top[None, :]), axis=0)]
    dot_general x4 -> x0, matrix products: 9.28 us -> none  [tile_cost(): inner = jnp.dot(sources, moving.T, preferred_element_type=jnp.float32)]
    all_gather x1 -> x0, blocking collectives: 7.53 us -> none  [local(): lax.all_gather(jnp.stack([potential, log_tgt]), 'blk', axis=1, tiled=True)]
    ppermute x3 -> x0, waiting for transfers between devices: 6.67 us -> none  [shifted(): return lax.ppermute(block, axis, route)]
    ppermute x3 -> x0, starting transfers between devices: 5.76 us -> none  [shifted(): return lax.ppermute(block, axis, route)]
  transfers between devices with their start and end apart: 3 -> 0, of which waited for: 2 -> 0; matrix products, arithmetic and copies ran while one was open for 8% -> 0% of each run, Pallas kernels for 0% -> 0%
where the time goes in v1:
time: 39.7 us; the launch traced here: 39.5 us
  Pallas kernels  36.3 us (91%)
  local copies, waits for them, and re-layouts  2.51 us (6%)
  between operations  0.64 us (2%)
    pallas_call x1, Pallas kernels, local(): pl.pallas_call(kernel, out_shape=[jax.ShapeDtypeStruct((ROWS // TILE, TIL...  36.3 us
    unnamed x2, local copies, waits for them, and re-layouts  2.51 us

profile of v1, /device:TPU:1, one launch (start us, length us, event | category | flops | bytes accessed | tf_op | source)
XLA Modules:
  0.0 39.5 jit_solution(14508945485663625468)
XLA Ops:
  0.6 36.3 %shard_map.68 = (f32[16,128]{1,0:T(8,128)}, f32[2,128]{1,0:T(2,128)}) custom-call(bf16[2048,1024]{1,0:T(8,128)(2,1)} %sources.1, bf16[256,1024]{1,0:T(8,128)(2,1)} %targets.1, f32[16,128]{1,0:T(8,128)} %bitcast.7, f32[2,128]{1,0:T(2,128)} %bitcast.8, f32[2,128]{1,0:T(2,128)} %bitcast.9), custom_call_target="tpu_custom_call" | custom-call | flops 4294967296 | bytes 6291456 | tf_op jit(solution)/shard_map/pallas_call | solution.py:310
  37.0 1.3 %copy.9 = f32[2048]{0:T(1024)} copy(f32[2048]{0:T(1024)} %bitcast.5) | data formatting | bytes 16384
  38.3 1.2 %copy.10 = f32[256]{0:T(256)} copy(f32[256]{0:T(256)} %bitcast.6) | data formatting | bytes 2048

commit v2 on v1

--- a/solution.py
+++ b/solution.py
@@ -32,6 +32,14 @@
         half = value.shape[1] // 2
         value = op(value[:, :half], value[:, half:])
     return value
+
+
+def line_hops(step):
+    return min(step, 2 * SIDE - step)
+
+
+def plane_hops(step):
+    return sum(min(n, SIDE - n) for n in divmod(step, SIDE))
 
 
 def kernel(
@@ -104,27 +112,24 @@
     ]
 
     barrier = pltpu.get_barrier_semaphore()
+    line_steps = sorted(range(1, 2 * SIDE), key=line_hops, reverse=True)
+    plane_steps = sorted(range(1, SIDE * SIDE), key=plane_hops, reverse=True)
 
     def greet(peers):
         for peer in peers:
             pl.semaphore_signal(barrier, inc=1, device_id=peer, device_id_type=MESH)
-        pl.semaphore_wait(barrier, len(peers))
+
+    lone = [sibling, above, below] + [line(n, 1) for n in line_steps] + [plane(n, 1) for n in plane_steps]
+    hub = [sibling] + [line(n, to) for n in line_steps for to in range(2)]
+    hub += [plane(n, to) for n in plane_steps for to in range(2)]
 
     @pl.when(core == 0)
     def _():
-        greet(
-            [sibling, above, below]
-            + [line(step, 1) for step in range(1, 2 * SIDE)]
-            + [plane(step, 1) for step in range(1, SIDE * SIDE)]
-        )
+        greet(lone)
 
     @pl.when(core == 1)
     def _():
-        greet(
-            [sibling]
-            + [line(step, to) for step in range(1, 2 * SIDE) for to in range(2)]
-            + [plane(step, to) for step in range(1, SIDE * SIDE) for to in range(2)]
-        )
+        greet(hub)
 
     sends = []
 
@@ -141,9 +146,39 @@
         sends.append(copy)
         return copy
 
+    core_rows = core * BLOCK
     load_t.wait()
-    core_rows = core * BLOCK
-    up, down, pass_up, pass_down = [], [], [], []
+    load_p.wait()
+    load_l.wait()
+    for half in range(2):
+        rows = pl.ds(pl.multiple_of(core_rows + half * TILE, TILE), TILE)
+        block = near_t[rows, :].astype(F32)
+        tgt_norms = jnp.sum(fold_lanes(jnp.add, block * block).T, axis=0, keepdims=True)
+        bias = bias_v[8 + half : 9 + half, :] + 2.0 * bias_v[half : half + 1, :]
+        row_bias[pl.ds(core * 2 + half, 1), :] = (bias - tgt_norms / 16.0) * LOG2E
+
+    def widen(slot):
+        for half in range(2):
+            row = jnp.broadcast_to(row_bias[pl.ds(slot * 2 + half, 1), :], (TILE, TILE))
+            wide_bias[pl.ds(pl.multiple_of(slot * BLOCK + half * TILE, TILE), TILE), :] = row.T
+
+    widen(core)
+    load_w.wait()
+    weights = jnp.concatenate([weight_v[n : n + 1, :] for n in range(ROWS // TILE)], axis=1)
+    shift[...] = jnp.broadcast_to(weights * LOG2E, (8, ROWS))
+
+    @pl.when(core == 0)
+    def _():
+        pl.semaphore_wait(barrier, len(lone))
+
+    @pl.when(core == 1)
+    def _():
+        pl.semaphore_wait(barrier, len(hub))
+
+    up, down = [], []
+    own_bias = row_bias.at[pl.ds(core * 2, 2)]
+    far_bias = row_bias.at[pl.ds(4 + core * 2, 2)]
+    bias_far = send(own_bias, far_bias, 4 * PIECES + 2, above)
     for piece in range(PIECES):
         low = pl.ds(pl.multiple_of(core_rows + piece * PART, PART), PART)
         high = pl.ds(pl.multiple_of(core_rows + BLOCK // 2 + piece * PART, PART), PART)
@@ -152,33 +187,18 @@
         up.append(send(near_t.at[low], far_t.at[piece, land_low], 4 * piece, above))
         down.append(send(near_t.at[high], far_t.at[piece, land_high], 4 * piece + 1, below))
     near = send(near_t.at[own_rows], near_t.at[own_rows], 4 * PIECES, sibling)
-
-    load_p.wait()
-    load_l.wait()
-    for half in range(2):
-        rows = pl.ds(pl.multiple_of(core_rows + half * TILE, TILE), TILE)
-        block = near_t[rows, :].astype(F32)
-        tgt_norms = jnp.sum(fold_lanes(jnp.add, block * block).T, axis=0, keepdims=True)
-        bias = bias_v[8 + half : 9 + half, :] + 2.0 * bias_v[half : half + 1, :]
-        row_bias[pl.ds(core * 2 + half, 1), :] = (bias - tgt_norms / 16.0) * LOG2E
     own_bias = row_bias.at[pl.ds(core * 2, 2)]
     far_bias = row_bias.at[pl.ds(4 + core * 2, 2)]
     bias_near = send(own_bias, own_bias, 4 * PIECES + 1, sibling)
-    bias_far = send(own_bias, far_bias, 4 * PIECES + 2, above)
-
-    def widen(slot):
-        for half in range(2):
-            row = jnp.broadcast_to(row_bias[pl.ds(slot * 2 + half, 1), :], (TILE, TILE))
-            wide_bias[pl.ds(pl.multiple_of(slot * BLOCK + half * TILE, TILE), TILE), :] = row.T
-
-    def row_pass(moving, segments, number, waits=()):
-        bias = [wide_bias[rows, :] for rows in segments]
-        bias = bias[0] if len(bias) == 1 else jnp.concatenate(bias, axis=0)
-        length = bias.shape[0] // len(segments)
-        for part in range(4):
+
+    def row_pass(moving, segments, parts, waits=()):
+        length = moving.shape[0] // len(segments)
+        for part in parts:
             if waits:
                 waits[part].wait()
-            inner = dot_t(moving, src_v[part * quarter : (part + 1) * quarter, :])
+            bias = [wide_bias[rows, :] for rows in segments]
+            bias = bias[0] if len(bias) == 1 else jnp.concatenate(bias, axis=0)
+            inner = dot_t(moving[...], src_v[part * quarter : (part + 1) * quarter, :])
             for tile in range(quarter // TILE):
                 lanes = pl.ds(part * quarter + tile * TILE, TILE)
                 value = inner[:, tile * TILE : (tile + 1) * TILE] * (LOG2E / 8.0) + bias
@@ -186,50 +206,57 @@
                     scores[rows, lanes] = value[at * length : (at + 1) * length, :]
                 deep = value.reshape(-1, 8, TILE)
                 top = jnp.max(deep, axis=0)
-                row_max[number * 8 : number * 8 + 8, lanes] = top
-                row_sum[number * 8 : number * 8 + 8, lanes] = jnp.sum(jnp.exp2(deep - top[None]), axis=0)
-
-    widen(core)
-    row_pass(near_t[own_rows, :], [own_rows], 0, load_s)
+                if waits:
+                    row_sum[:, lanes] = jnp.sum(jnp.exp2(deep - top[None]), axis=0)
+                else:
+                    before = row_max[:, lanes]
+                    top = jnp.maximum(top, before)
+                    row_sum[:, lanes] = row_sum[:, lanes] * jnp.exp2(before - top) + jnp.sum(
+                        jnp.exp2(deep - top[None]), axis=0
+                    )
+                row_max[:, lanes] = top
+
+    row_pass(near_t.at[own_rows], [own_rows], range(4), load_s)
     near.wait_recv()
     bias_near.wait_recv()
     widen(1 - core)
-    row_pass(near_t[sib_rows, :], [sib_rows], 1)
-
+    row_pass(near_t.at[sib_rows], [sib_rows], range(4))
+
+    for tile in range(ROWS // TILE):
+        block = src_v[tile * TILE : (tile + 1) * TILE, :].astype(F32)
+        norms[tile : tile + 1, :] = jnp.sum(fold_lanes(jnp.add, block * block).T, axis=0, keepdims=True)
     bias_far.wait_recv()
     bias_pass = send(far_bias, far_bias, 4 * PIECES + 3, sibling)
-    for piece in range(PIECES):
+
+    def pass_on(piece):
         up[piece].wait_recv()
         down[piece].wait_recv()
         land = far_t.at[piece, pl.ds(pl.multiple_of(core * 2 * PART, 2 * PART), 2 * PART)]
-        passed = send(land, land, 4 * piece + 2, sibling)
-        if piece == 0:
-            for tile in range(ROWS // TILE):
-                block = src_v[tile * TILE : (tile + 1) * TILE, :].astype(F32)
-                norms[tile : tile + 1, :] = jnp.sum(fold_lanes(jnp.add, block * block).T, axis=0, keepdims=True)
-            bias_pass.wait_recv()
-            widen(2)
-            widen(3)
-        passed.wait_recv()
+        return send(land, land, 4 * piece + 2, sibling)
+
+    passed = pass_on(0)
+    bias_pass.wait_recv()
+    widen(2)
+    widen(3)
+    for piece in range(PIECES):
         segments = [
             pl.ds(2 * BLOCK + of_core * BLOCK + half * (BLOCK // 2) + piece * PART, PART)
             for of_core in range(2)
             for half in range(2)
         ]
-        row_pass(far_t[piece], segments, 2 + piece)
-
-    load_w.wait()
-    peaks = row_max[...].reshape(2 + PIECES, 8, ROWS)
-    peak = jnp.max(peaks, axis=0)
-    total = jnp.sum(row_sum[...].reshape(2 + PIECES, 8, ROWS) * jnp.exp2(peaks - peak[None]), axis=0)
+        passed.wait_recv()
+        if piece + 1 < PIECES:
+            row_pass(far_t.at[piece], segments, range(2))
+            passed = pass_on(piece + 1)
+            row_pass(far_t.at[piece], segments, range(2, 4))
+        else:
+            row_pass(far_t.at[piece], segments, range(4))
+
+    peak, total = row_max[...], row_sum[...]
     top = jnp.max(peak, axis=0, keepdims=True)
     row_log = top + jnp.log2(jnp.sum(total * jnp.exp2(peak - top), axis=0, keepdims=True))
-    weights = jnp.concatenate([weight_v[n : n + 1, :] for n in range(ROWS // TILE)], axis=1)
-    shift[...] = jnp.broadcast_to(weights * LOG2E - row_log, (8, ROWS))
-    for tile in range(ROWS // TILE):
-        src_out[tile : tile + 1, :] = (
-            norms[tile : tile + 1, :] / 32.0 - 64.0 - (0.5 * LN2) * row_log[:, tile * TILE : (tile + 1) * TILE]
-        )
+    shift[...] = shift[...] - row_log
+    row_max[0:1, :] = row_log
 
     for block in range(COLS // TILE):
         for group in range(TILE // 8):
@@ -271,11 +298,17 @@
         top = functools.reduce(jnp.maximum, [peak[p] for p in parts])
         return top + jnp.log2(sum(total[p] * jnp.exp2(peak[p] - top) for p in parts))
 
-    for step in range(1, 2 * SIDE):
+    for step in line_steps:
         part = col_log.at[4 * (step % 2) : 4 * (step % 2) + 4]
         slot = pl.ds(pl.multiple_of(8 * step + 4 * core, 4), 4)
         reduce_send(part, line_in.at[slot], 0, line(step, 1))
 
+    for tile in range(ROWS // TILE):
+        lanes = pl.ds(tile * TILE, TILE)
+        src_out[lanes] = (
+            norms[tile : tile + 1, :] / 32.0 - 64.0 - (0.5 * LN2) * row_max[0:1, lanes]
+        ).reshape(TILE)
+
     @pl.when(core == 0)
     def _():
         reduce_send(col_log.at[0:4], line_in.at[0:4], 0, sibling)
@@ -287,7 +320,7 @@
         line_in[4:8, :] = col_log[0:4, :]
         arrived(line_in.at[0:60], 0)
         line_out[0:4, :] = merge(line_in[...], 4)
-        for step in range(1, SIDE * SIDE):
+        for step in plane_steps:
             for to in range(2):
                 reduce_send(
                     line_out.at[2 * to : 2 * to + 2], plane_in.at[2 * step : 2 * step + 2], 1, plane(step, to)
@@ -298,10 +331,21 @@
         left(line_in.at[0:28], 0)
         left(line_in.at[0:62], 1)
 
-    tgt_out[...] = bias_v[0:2, :] + 0.5 * bias_v[8:10, :] - (0.5 * LN2) * merge(plane_in[...], 2)
+    tgt_new = bias_v[0:2, :] + 0.5 * bias_v[8:10, :] - (0.5 * LN2) * merge(plane_in[...], 2)
+    for half in range(2):
+        tgt_out[half * TILE : (half + 1) * TILE] = tgt_new[half : half + 1, :].reshape(TILE)
 
     for copy in sends:
         copy.wait_send()
+
+
+def finish(src_in, tgt_in, src_out, tgt_out, sem):
+    one = pltpu.make_async_copy(src_in, src_out, sem.at[0])
+    two = pltpu.make_async_copy(tgt_in, tgt_out, sem.at[1])
+    one.start()
+    two.start()
+    one.wait()
+    two.wait()
 
 
 def local(sources, targets, log_src, log_tgt, potential):
@@ -310,8 +354,8 @@
     src_out, tgt_out = pl.pallas_call(
         kernel,
         out_shape=[
-            jax.ShapeDtypeStruct((ROWS // TILE, TILE), F32),
-            jax.ShapeDtypeStruct((BLOCK // TILE, TILE), F32),
+            pltpu.VMEM((ROWS,), F32),
+            pltpu.VMEM((BLOCK,), F32),
         ],
         in_specs=[anywhere] * 5,
         out_specs=[vmem] * 2,
@@ -325,8 +369,8 @@
             pltpu.VMEM((COLS, TILE), F32),
             pltpu.VMEM((ROWS // TILE, TILE), F32),
             pltpu.VMEM((COLS, ROWS), F32),
-            pltpu.VMEM((8 * (2 + PIECES), ROWS), F32),
-            pltpu.VMEM((8 * (2 + PIECES), ROWS), F32),
+            pltpu.VMEM((8, ROWS), F32),
+            pltpu.VMEM((8, ROWS), F32),
             pltpu.VMEM((8, ROWS), F32),
             pltpu.VMEM((COLS, TILE), F32),
             pltpu.VMEM((COLS, TILE), F32),
@@ -354,7 +398,16 @@
         log_tgt.reshape(BLOCK // TILE, TILE),
         potential.reshape(BLOCK // TILE, TILE),
     )
-    return src_out.reshape(ROWS), tgt_out.reshape(BLOCK)
+    return pl.pallas_call(
+        finish,
+        out_shape=[jax.ShapeDtypeStruct((ROWS,), F32), jax.ShapeDtypeStruct((BLOCK,), F32)],
+        in_specs=[vmem] * 2,
+        out_specs=[anywhere] * 2,
+        scratch_shapes=[pltpu.SemaphoreType.DMA((2,))],
+    )(
+        pltpu.with_memory_space_constraint(src_out, pltpu.VMEM),
+        pltpu.with_memory_space_constraint(tgt_out, pltpu.VMEM),
+    )
 
 
 def solution(mesh):

time: 39.7 us -> 33.9 us (0.85)
  Pallas kernels: 36.3 us -> 33.2 us
  local copies, waits for them, and re-layouts: 2.51 us -> 0 us
    pallas_call x1 -> x2, Pallas kernels: 36.3 us -> 33.2 us  [the longest x1 32.5 us: local(): pl.pallas_call(kernel, out_shape=[pltpu.VMEM((ROWS,), F32), pltpu.VMEM((B...]
    unnamed x2 -> x0, local copies, waits for them, and re-layouts: 2.51 us -> none
where the time goes in v2:
time: 33.9 us; the launch traced here: 33.8 us
  Pallas kernels  33.2 us (98%)
  between operations  0.64 us (2%)
    pallas_call x1, Pallas kernels, local(): pl.pallas_call(kernel, out_shape=[pltpu.VMEM((ROWS,), F32), pltpu.VMEM((B...  32.5 us

profile of v2, /device:TPU:1, one launch (start us, length us, event | category | flops | bytes accessed | tf_op | source)
XLA Modules:
  0.0 33.8 jit_solution(7685874491498494460)
XLA Ops:
  0.6 32.5 %shard_map.68 = (f32[2048]{0:T(1024)S(1)}, f32[256]{0:T(256)S(1)}) custom-call(bf16[2048,1024]{1,0:T(8,128)(2,1)} %sources.1, bf16[256,1024]{1,0:T(8,128)(2,1)} %targets.1, f32[16,128]{1,0:T(8,128)} %bitcast.3, f32[2,128]{1,0:T(2,128)} %bitcast.4, f32[2,128]{1,0:T(2,128)} %bitcast.5), custom_call_target="tpu_custom_call" | custom-call | flops 4294967296 | bytes 6291456 | tf_op jit(solution)/shard_map/pallas_call | solution.py:354
  33.2 0.6 %shard_map.69 = (f32[2048]{0:T(1024)}, f32[256]{0:T(256)}) custom-call(f32[2048]{0:T(1024)S(1)} %get-tuple-element.4.src_in, f32[256]{0:T(256)S(1)} %get-tuple-element.5.tgt_in), custom_call_target="tpu_custom_call" | custom-call | tf_op jit(solution)/shard_map/pallas_call | solution.py:401

commit v3 on v2

--- a/solution.py
+++ b/solution.py
@@ -72,6 +72,7 @@
     send_sem,
     recv_sem,
     reduce_sem,
+    news_sem,
 ):
     src = lax.axis_index("src")
     blk = lax.axis_index("blk")
@@ -119,9 +120,10 @@
         for peer in peers:
             pl.semaphore_signal(barrier, inc=1, device_id=peer, device_id_type=MESH)
 
-    lone = [sibling, above, below] + [line(n, 1) for n in line_steps] + [plane(n, 1) for n in plane_steps]
-    hub = [sibling] + [line(n, to) for n in line_steps for to in range(2)]
-    hub += [plane(n, to) for n in plane_steps for to in range(2)]
+    x_sides = [plane(n * SIDE, 1) for n in (1, SIDE - 1)]
+    y_sides = [plane(n, 1) for n in (1, SIDE - 1)]
+    lone = [sibling, above, below]
+    hub = lone + x_sides + y_sides
 
     @pl.when(core == 0)
     def _():
@@ -190,6 +192,18 @@
     own_bias = row_bias.at[pl.ds(core * 2, 2)]
     far_bias = row_bias.at[pl.ds(4 + core * 2, 2)]
     bias_near = send(own_bias, own_bias, 4 * PIECES + 1, sibling)
+
+    def news(number, amount):
+        pl.semaphore_wait(news_sem.at[number], amount)
+
+    def tell(number, peers):
+        for peer in peers:
+            pl.semaphore_signal(news_sem.at[number], inc=1, device_id=peer, device_id_type=MESH)
+
+    @pl.when(core == 1)
+    def _():
+        tell(0, [above, below])
+        tell(1, x_sides)
 
     def row_pass(moving, segments, parts, waits=()):
         length = moving.shape[0] // len(segments)
@@ -222,6 +236,13 @@
     widen(1 - core)
     row_pass(near_t.at[sib_rows], [sib_rows], range(4))
 
+    @pl.when(core == 1)
+    def _():
+        news(0, 2)
+        news(1, 2)
+        tell(2, [line(2, 1), line(2 * SIDE - 2, 1)])
+        tell(3, [plane(2 * SIDE, 1)])
+
     for tile in range(ROWS // TILE):
         block = src_v[tile * TILE : (tile + 1) * TILE, :].astype(F32)
         norms[tile : tile + 1, :] = jnp.sum(fold_lanes(jnp.add, block * block).T, axis=0, keepdims=True)
@@ -235,6 +256,14 @@
         return send(land, land, 4 * piece + 2, sibling)
 
     passed = pass_on(0)
+
+    @pl.when(core == 1)
+    def _():
+        news(2, 2)
+        news(3, 1)
+        tell(4, [sibling])
+        tell(5, y_sides)
+
     bias_pass.wait_recv()
     widen(2)
     widen(3)
@@ -248,6 +277,12 @@
         if piece + 1 < PIECES:
             row_pass(far_t.at[piece], segments, range(2))
             passed = pass_on(piece + 1)
+
+            @pl.when(core == 1)
+            def _():
+                news(5, 2)
+                tell(6, [plane(SIDE // 2, 1)])
+
             row_pass(far_t.at[piece], segments, range(2, 4))
         else:
             row_pass(far_t.at[piece], segments, range(4))
@@ -298,6 +333,10 @@
         top = functools.reduce(jnp.maximum, [peak[p] for p in parts])
         return top + jnp.log2(sum(total[p] * jnp.exp2(peak[p] - top) for p in parts))
 
+    @pl.when(core == 0)
+    def _():
+        news(4, 1)
+
     for step in line_steps:
         part = col_log.at[4 * (step % 2) : 4 * (step % 2) + 4]
         slot = pl.ds(pl.multiple_of(8 * step + 4 * core, 4), 4)
@@ -320,6 +359,7 @@
         line_in[4:8, :] = col_log[0:4, :]
         arrived(line_in.at[0:60], 0)
         line_out[0:4, :] = merge(line_in[...], 4)
+        news(6, 1)
         for step in plane_steps:
             for to in range(2):
                 reduce_send(
@@ -382,6 +422,7 @@
             pltpu.SemaphoreType.DMA((4 * PIECES + 4,)),
             pltpu.SemaphoreType.DMA((4 * PIECES + 4,)),
             pltpu.SemaphoreType.DMA((4,)),
+            pltpu.SemaphoreType.REGULAR((7,)),
         ],
         compiler_params=pltpu.CompilerParams(
             collective_id=0, has_side_effects=True, vmem_limit_bytes=56 * 2**20

time: 33.9 us -> 32.6 us (0.962)
  Pallas kernels: 33.2 us -> 31.8 us
    pallas_call x1, Pallas kernels: 32.5 us -> 31.2 us  [local(): pl.pallas_call(kernel, out_shape=[pltpu.VMEM((ROWS,), F32), pltpu.VMEM((B...]
where the time goes in v3:
time: 32.6 us; the launch traced here: 32.5 us
  Pallas kernels  31.8 us (98%)
  between operations  0.64 us (2%)
    pallas_call x1, Pallas kernels, local(): pl.pallas_call(kernel, out_shape=[pltpu.VMEM((ROWS,), F32), pltpu.VMEM((B...  31.2 us

profile of v3, /device:TPU:1, one launch (start us, length us, event | category | flops | bytes accessed | tf_op | source)
XLA Modules:
  0.0 32.5 jit_solution(16953111471633375870)
XLA Ops:
  0.6 31.2 %shard_map.68 = (f32[2048]{0:T(1024)S(1)}, f32[256]{0:T(256)S(1)}) custom-call(bf16[2048,1024]{1,0:T(8,128)(2,1)} %sources.1, bf16[256,1024]{1,0:T(8,128)(2,1)} %targets.1, f32[16,128]{1,0:T(8,128)} %bitcast.3, f32[2,128]{1,0:T(2,128)} %bitcast.4, f32[2,128]{1,0:T(2,128)} %bitcast.5), custom_call_target="tpu_custom_call" | custom-call | flops 4294967296 | bytes 6291456 | tf_op jit(solution)/shard_map/pallas_call | solution.py:394
  31.9 0.6 %shard_map.69 = (f32[2048]{0:T(1024)}, f32[256]{0:T(256)}) custom-call(f32[2048]{0:T(1024)S(1)} %get-tuple-element.4.src_in, f32[256]{0:T(256)S(1)} %get-tuple-element.5.tgt_in), custom_call_target="tpu_custom_call" | custom-call | tf_op jit(solution)/shard_map/pallas_call | solution.py:442

commit v4 on v3

--- a/solution.py
+++ b/solution.py
@@ -275,7 +275,7 @@
         ]
         passed.wait_recv()
         if piece + 1 < PIECES:
-            row_pass(far_t.at[piece], segments, range(2))
+            row_pass(far_t.at[piece], segments, range(1))
             passed = pass_on(piece + 1)
 
             @pl.when(core == 1)
@@ -283,7 +283,7 @@
                 news(5, 2)
                 tell(6, [plane(SIDE // 2, 1)])
 
-            row_pass(far_t.at[piece], segments, range(2, 4))
+            row_pass(far_t.at[piece], segments, range(1, 4))
         else:
             row_pass(far_t.at[piece], segments, range(4))
 
@@ -292,20 +292,6 @@
     row_log = top + jnp.log2(jnp.sum(total * jnp.exp2(peak - top), axis=0, keepdims=True))
     shift[...] = shift[...] - row_log
     row_max[0:1, :] = row_log
-
-    for block in range(COLS // TILE):
-        for group in range(TILE // 8):
-            rows = pl.ds(block * TILE + group * 8, 8)
-            value = scores[rows, :] + shift[...]
-            peak = fold_lanes(jnp.maximum, value)
-            deep = jnp.concatenate([peak] * (ROWS // TILE), axis=1)
-            col_max[rows, :] = peak
-            col_sum[rows, :] = fold_lanes(jnp.add, jnp.exp2(value - deep))
-        rows = pl.ds(block * TILE, TILE)
-        peaks = col_max[rows, :].T
-        peak = jnp.max(peaks, axis=0, keepdims=True)
-        total = jnp.sum(col_sum[rows, :].T * jnp.exp2(peaks - peak), axis=0, keepdims=True)
-        col_log[block : block + 1, :] = peak + jnp.log2(total)
 
     def reduce_send(from_ref, to_ref, stage, peer):
         copy = pltpu.make_async_remote_copy(
@@ -333,14 +319,35 @@
         top = functools.reduce(jnp.maximum, [peak[p] for p in parts])
         return top + jnp.log2(sum(total[p] * jnp.exp2(peak[p] - top) for p in parts))
 
+    def column_pass(blocks):
+        for block in blocks:
+            for group in range(TILE // 8):
+                rows = pl.ds(block * TILE + group * 8, 8)
+                value = scores[rows, :] + shift[...]
+                peak = fold_lanes(jnp.maximum, value)
+                deep = jnp.concatenate([peak] * (ROWS // TILE), axis=1)
+                col_max[rows, :] = peak
+                col_sum[rows, :] = fold_lanes(jnp.add, jnp.exp2(value - deep))
+            rows = pl.ds(block * TILE, TILE)
+            peaks = col_max[rows, :].T
+            peak = jnp.max(peaks, axis=0, keepdims=True)
+            total = jnp.sum(col_sum[rows, :].T * jnp.exp2(peaks - peak), axis=0, keepdims=True)
+            col_log[block : block + 1, :] = peak + jnp.log2(total)
+
     @pl.when(core == 0)
     def _():
         news(4, 1)
 
-    for step in line_steps:
-        part = col_log.at[4 * (step % 2) : 4 * (step % 2) + 4]
-        slot = pl.ds(pl.multiple_of(8 * step + 4 * core, 4), 4)
-        reduce_send(part, line_in.at[slot], 0, line(step, 1))
+    for parity in range(2):
+        column_pass(range(4 * parity, 4 * parity + 4))
+        for step in line_steps:
+            if step % 2 == parity:
+                slot = pl.ds(pl.multiple_of(8 * step + 4 * core, 4), 4)
+                reduce_send(col_log.at[4 * parity : 4 * parity + 4], line_in.at[slot], 0, line(step, 1))
+
+    @pl.when(core == 0)
+    def _():
+        reduce_send(col_log.at[0:4], line_in.at[0:4], 0, sibling)
 
     for tile in range(ROWS // TILE):
         lanes = pl.ds(tile * TILE, TILE)
@@ -350,7 +357,6 @@
 
     @pl.when(core == 0)
     def _():
-        reduce_send(col_log.at[0:4], line_in.at[0:4], 0, sibling)
         arrived(plane_in, 1)
         left(line_in.at[0:32], 0)
 

time: 32.6 us -> 31.5 us (0.966)
  Pallas kernels: 31.8 us -> 30.8 us
    pallas_call x1, Pallas kernels: 31.2 us -> 30.1 us  [local(): pl.pallas_call(kernel, out_shape=[pltpu.VMEM((ROWS,), F32), pltpu.VMEM((B...]
where the time goes in v4:
time: 31.5 us; the launch traced here: 31.4 us
  Pallas kernels  30.8 us (98%)
  between operations  0.64 us (2%)
    pallas_call x1, Pallas kernels, local(): pl.pallas_call(kernel, out_shape=[pltpu.VMEM((ROWS,), F32), pltpu.VMEM((B...  30.1 us

profile of v4, /device:TPU:1, one launch (start us, length us, event | category | flops | bytes accessed | tf_op | source)
XLA Modules:
  0.0 31.4 jit_solution(4231946326837253078)
XLA Ops:
  0.6 30.1 %shard_map.68 = (f32[2048]{0:T(1024)S(1)}, f32[256]{0:T(256)S(1)}) custom-call(bf16[2048,1024]{1,0:T(8,128)(2,1)} %sources.1, bf16[256,1024]{1,0:T(8,128)(2,1)} %targets.1, f32[16,128]{1,0:T(8,128)} %bitcast.3, f32[2,128]{1,0:T(2,128)} %bitcast.4, f32[2,128]{1,0:T(2,128)} %bitcast.5), custom_call_target="tpu_custom_call" | custom-call | flops 4294967296 | bytes 6291456 | tf_op jit(solution)/shard_map/pallas_call | solution.py:400
  30.8 0.6 %shard_map.69 = (f32[2048]{0:T(1024)}, f32[256]{0:T(256)}) custom-call(f32[2048]{0:T(1024)S(1)} %get-tuple-element.4.src_in, f32[256]{0:T(256)S(1)} %get-tuple-element.5.tgt_in), custom_call_target="tpu_custom_call" | custom-call | tf_op jit(solution)/shard_map/pallas_call | solution.py:448

commit v5 on v4

--- a/solution.py
+++ b/solution.py
@@ -181,6 +181,8 @@
     own_bias = row_bias.at[pl.ds(core * 2, 2)]
     far_bias = row_bias.at[pl.ds(4 + core * 2, 2)]
     bias_far = send(own_bias, far_bias, 4 * PIECES + 2, above)
+    bias_near = send(own_bias, own_bias, 4 * PIECES + 1, sibling)
+    near = send(near_t.at[own_rows], near_t.at[own_rows], 4 * PIECES, sibling)
     for piece in range(PIECES):
         low = pl.ds(pl.multiple_of(core_rows + piece * PART, PART), PART)
         high = pl.ds(pl.multiple_of(core_rows + BLOCK // 2 + piece * PART, PART), PART)
@@ -188,10 +190,8 @@
         land_high = pl.ds(pl.multiple_of(core * 2 * PART + PART, PART), PART)
         up.append(send(near_t.at[low], far_t.at[piece, land_low], 4 * piece, above))
         down.append(send(near_t.at[high], far_t.at[piece, land_high], 4 * piece + 1, below))
-    near = send(near_t.at[own_rows], near_t.at[own_rows], 4 * PIECES, sibling)
     own_bias = row_bias.at[pl.ds(core * 2, 2)]
     far_bias = row_bias.at[pl.ds(4 + core * 2, 2)]
-    bias_near = send(own_bias, own_bias, 4 * PIECES + 1, sibling)
 
     def news(number, amount):
         pl.semaphore_wait(news_sem.at[number], amount)
@@ -243,9 +243,6 @@
         tell(2, [line(2, 1), line(2 * SIDE - 2, 1)])
         tell(3, [plane(2 * SIDE, 1)])
 
-    for tile in range(ROWS // TILE):
-        block = src_v[tile * TILE : (tile + 1) * TILE, :].astype(F32)
-        norms[tile : tile + 1, :] = jnp.sum(fold_lanes(jnp.add, block * block).T, axis=0, keepdims=True)
     bias_far.wait_recv()
     bias_pass = send(far_bias, far_bias, 4 * PIECES + 3, sibling)
 
@@ -350,6 +347,9 @@
         reduce_send(col_log.at[0:4], line_in.at[0:4], 0, sibling)
 
     for tile in range(ROWS // TILE):
+        block = src_v[tile * TILE : (tile + 1) * TILE, :].astype(F32)
+        norms[tile : tile + 1, :] = jnp.sum(fold_lanes(jnp.add, block * block).T, axis=0, keepdims=True)
+    for tile in range(ROWS // TILE):
         lanes = pl.ds(tile * TILE, TILE)
         src_out[lanes] = (
             norms[tile : tile + 1, :] / 32.0 - 64.0 - (0.5 * LN2) * row_max[0:1, lanes]
@@ -358,7 +358,6 @@
     @pl.when(core == 0)
     def _():
         arrived(plane_in, 1)
-        left(line_in.at[0:32], 0)
 
     @pl.when(core == 1)
     def _():
@@ -366,16 +365,14 @@
         arrived(line_in.at[0:60], 0)
         line_out[0:4, :] = merge(line_in[...], 4)
         news(6, 1)
-        for step in plane_steps:
-            for to in range(2):
+        for to in (1, 0):
+            for step in plane_steps:
                 reduce_send(
                     line_out.at[2 * to : 2 * to + 2], plane_in.at[2 * step : 2 * step + 2], 1, plane(step, to)
                 )
         reduce_send(line_out.at[0:2], plane_in.at[0:2], 1, sibling)
         plane_in[0:2, :] = line_out[2:4, :]
         arrived(plane_in.at[2:32], 1)
-        left(line_in.at[0:28], 0)
-        left(line_in.at[0:62], 1)
 
     tgt_new = bias_v[0:2, :] + 0.5 * bias_v[8:10, :] - (0.5 * LN2) * merge(plane_in[...], 2)
     for half in range(2):
@@ -383,6 +380,15 @@
 
     for copy in sends:
         copy.wait_send()
+
+    @pl.when(core == 0)
+    def _():
+        left(line_in.at[0:32], 0)
+
+    @pl.when(core == 1)
+    def _():
+        left(line_in.at[0:28], 0)
+        left(line_in.at[0:62], 1)
 
 
 def finish(src_in, tgt_in, src_out, tgt_out, sem):

time: 31.5 us -> 31.2 us (level)
  no operation moved by 1% of the time
where the time goes in v5:
time: 31.2 us
  Pallas kernels  30.5 us (98%)
  between operations  0.64 us (2%)
    pallas_call x1, Pallas kernels, local(): pl.pallas_call(kernel, out_shape=[pltpu.VMEM((ROWS,), F32), pltpu.VMEM((B...  29.9 us

profile of v5, /device:TPU:1, one launch (start us, length us, event | category | flops | bytes accessed | tf_op | source)
XLA Modules:
  0.0 31.2 jit_solution(14933421521111840332)
XLA Ops:
  0.6 29.9 %shard_map.68 = (f32[2048]{0:T(1024)S(1)}, f32[256]{0:T(256)S(1)}) custom-call(bf16[2048,1024]{1,0:T(8,128)(2,1)} %sources.1, bf16[256,1024]{1,0:T(8,128)(2,1)} %targets.1, f32[16,128]{1,0:T(8,128)} %bitcast.3, f32[2,128]{1,0:T(2,128)} %bitcast.4, f32[2,128]{1,0:T(2,128)} %bitcast.5), custom_call_target="tpu_custom_call" | custom-call | flops 4294967296 | bytes 6291456 | tf_op jit(solution)/shard_map/pallas_call | solution.py:406
  30.5 0.6 %shard_map.69 = (f32[2048]{0:T(1024)}, f32[256]{0:T(256)}) custom-call(f32[2048]{0:T(1024)S(1)} %get-tuple-element.4.src_in, f32[256]{0:T(256)S(1)} %get-tuple-element.5.tgt_in), custom_call_target="tpu_custom_call" | custom-call | tf_op jit(solution)/shard_map/pallas_call | solution.py:454

commit v6 on v5

--- a/solution.py
+++ b/solution.py
@@ -346,17 +346,19 @@
     def _():
         reduce_send(col_log.at[0:4], line_in.at[0:4], 0, sibling)
 
-    for tile in range(ROWS // TILE):
-        block = src_v[tile * TILE : (tile + 1) * TILE, :].astype(F32)
-        norms[tile : tile + 1, :] = jnp.sum(fold_lanes(jnp.add, block * block).T, axis=0, keepdims=True)
-    for tile in range(ROWS // TILE):
-        lanes = pl.ds(tile * TILE, TILE)
-        src_out[lanes] = (
-            norms[tile : tile + 1, :] / 32.0 - 64.0 - (0.5 * LN2) * row_max[0:1, lanes]
-        ).reshape(TILE)
-
-    @pl.when(core == 0)
-    def _():
+    def source_result():
+        for tile in range(ROWS // TILE):
+            block = src_v[tile * TILE : (tile + 1) * TILE, :].astype(F32)
+            norms[tile : tile + 1, :] = jnp.sum(fold_lanes(jnp.add, block * block).T, axis=0, keepdims=True)
+        for tile in range(ROWS // TILE):
+            lanes = pl.ds(tile * TILE, TILE)
+            src_out[lanes] = (
+                norms[tile : tile + 1, :] / 32.0 - 64.0 - (0.5 * LN2) * row_max[0:1, lanes]
+            ).reshape(TILE)
+
+    @pl.when(core == 0)
+    def _():
+        source_result()
         arrived(plane_in, 1)
 
     @pl.when(core == 1)
@@ -372,6 +374,7 @@
                 )
         reduce_send(line_out.at[0:2], plane_in.at[0:2], 1, sibling)
         plane_in[0:2, :] = line_out[2:4, :]
+        source_result()
         arrived(plane_in.at[2:32], 1)
 
     tgt_new = bias_v[0:2, :] + 0.5 * bias_v[8:10, :] - (0.5 * LN2) * merge(plane_in[...], 2)

time: 31.2 us -> 31.3 us (level)
  no operation moved by 1% of the time
where the time goes in v6:
time: 31.3 us
  Pallas kernels  30.6 us (98%)
  between operations  0.64 us (2%)
    pallas_call x1, Pallas kernels, local(): pl.pallas_call(kernel, out_shape=[pltpu.VMEM((ROWS,), F32), pltpu.VMEM((B...  30 us

profile of v6, /device:TPU:1, one launch (start us, length us, event | category | flops | bytes accessed | tf_op | source)
XLA Modules:
  0.0 31.3 jit_solution(254655997871516575)
XLA Ops:
  0.6 30.0 %shard_map.68 = (f32[2048]{0:T(1024)S(1)}, f32[256]{0:T(256)S(1)}) custom-call(bf16[2048,1024]{1,0:T(8,128)(2,1)} %sources.1, bf16[256,1024]{1,0:T(8,128)(2,1)} %targets.1, f32[16,128]{1,0:T(8,128)} %bitcast.3, f32[2,128]{1,0:T(2,128)} %bitcast.4, f32[2,128]{1,0:T(2,128)} %bitcast.5), custom_call_target="tpu_custom_call" | custom-call | flops 4294967296 | bytes 6291456 | tf_op jit(solution)/shard_map/pallas_call | solution.py:409
  30.6 0.6 %shard_map.69 = (f32[2048]{0:T(1024)}, f32[256]{0:T(256)}) custom-call(f32[2048]{0:T(1024)S(1)} %get-tuple-element.4.src_in, f32[256]{0:T(256)S(1)} %get-tuple-element.5.tgt_in), custom_call_target="tpu_custom_call" | custom-call | tf_op jit(solution)/shard_map/pallas_call | solution.py:457
